TPU v7x, 32 devices: a whole 2x2x4 slice. The times are simulated.
32 devices in a mesh: tile: 8 (over y, x, core), head: 4 (over z).
Axes of the slice: x: 2, y: 2, z: 4, core: 2. Of those that a mesh axis runs over, the one named last changes fastest.
Arguments:
- bott: bfloat16 [16, 128, 1024], P('tile', 'head'), may hold values from -10 to 10
- norm_gain: float32 [1024], replicated, may hold values from 0.1 to 1.9
- w_qkv: bfloat16 [3, 1024, 1024], P(None, None, 'head'), may hold values from -1 to 1
- w_out: bfloat16 [1024, 1024], P('head'), may hold values from -3 to 3
- dw_weight: float32 [3, 3, 1024], replicated, may hold values from -2 to 2
- join_bias: float32 [1024], replicated, may hold values from -3 to 3
- w_join: bfloat16 [1024, 1024], replicated, may hold values from -0.1875 to 0.1875
Outputs:
- joined: bfloat16 [16, 128, 1024], P('tile', 'head')
All inputs are finite; a program needn't handle non-finite values.
Results may differ from a plain program's by a relative error of at most 0.02.
Values may be sent and summed in bfloat16 or wider, within the bound.
A program may use at most 128 MiB of HBM per device.

v0:
```python
import math

import jax
import jax.numpy as jnp
from jax import lax
from jax.sharding import PartitionSpec as P

HEADS = 16


def with_halo(x, sides, width):
    for axis, dim in sides:
        size, length = (lax.axis_size(axis), x.shape[dim])
        up = [(i, (i + 1) % size) for i in range(size - 1)]
        down = [(j, i) for i, j in up]
        last = lax.slice_in_dim(x, length - width, length, axis=dim)
        leading = lax.slice_in_dim(x, 0, width, axis=dim)
        before = lax.ppermute(last, axis, up)
        after = lax.ppermute(leading, axis, down)
        x = jnp.concatenate([before, x, after], axis=dim)
    return x


def fold_blocks(state, queries, key_piece, value_piece, scale):
    count, heads_here, head_dim = key_piece.shape
    block = math.gcd(count, 2048)
    key_blocks = key_piece.reshape(count // block, block, heads_here, head_dim)
    value_blocks = value_piece.reshape(count // block, block, heads_here, head_dim)

    def one_block(inner, pair):
        maxes, totals, summed = inner
        key_block, value_block = pair
        scores = (
            jnp.einsum("qhe,khe->hqk", queries, key_block, preferred_element_type=jnp.float32)
            * scale
        )
        new_max = jnp.maximum(maxes, jnp.max(scores, axis=-1))
        weights = jnp.exp(scores - new_max[..., None])
        decay = jnp.exp(maxes - new_max)
        totals = totals * decay + jnp.sum(weights, axis=-1)
        summed = summed * decay[..., None] + jnp.einsum(
            "hqk,khe->hqe",
            weights.astype(jnp.bfloat16),
            value_block,
            preferred_element_type=jnp.float32,
        )
        return ((new_max, totals, summed), None)

    return lax.scan(one_block, state, (key_blocks, value_blocks))[0]


def empty_state(heads_here, query_count, head_dim):
    return (
        jnp.full((heads_here, query_count), -1e30, jnp.float32),
        jnp.zeros((heads_here, query_count), jnp.float32),
        jnp.zeros((heads_here, query_count, head_dim), jnp.float32),
    )


def per_device(bott, norm_gain, w_qkv, w_out, dw_weight, join_bias, w_join):
    rows, cols_dev, width = bott.shape
    values = bott.astype(jnp.float32)
    normed = (
        values * lax.rsqrt(jnp.mean(values * values, axis=-1, keepdims=True) + 1e-06) * norm_gain
    ).astype(jnp.bfloat16)
    all_heads = jnp.einsum(
        "rcd,jde->jcre",
        normed,
        lax.all_gather(w_qkv, "head", axis=2, tiled=True),
        preferred_element_type=jnp.float32,
    ).astype(jnp.bfloat16)
    projected = lax.all_to_all(all_heads, "head", split_axis=3, concat_axis=1, tiled=True)
    columns = projected.shape[1]
    local_width = projected.shape[3]
    head_dim = width // HEADS
    local_heads = local_width // head_dim
    seq_local = columns * rows
    scale = 1.0 / head_dim**0.5
    queries = projected[0].reshape(seq_local, local_heads, head_dim)
    keys = projected[1].reshape(seq_local, local_width)
    vals = projected[2].reshape(seq_local, local_width)
    start_state = empty_state(local_heads, seq_local, head_dim)
    key_piece = lax.all_gather(keys, "tile", axis=0, tiled=True)
    value_piece = lax.all_gather(vals, "tile", axis=0, tiled=True)
    count = key_piece.shape[0]
    maxes, totals, summed = fold_blocks(
        start_state,
        queries,
        key_piece.reshape(count, local_heads, head_dim),
        value_piece.reshape(count, local_heads, head_dim),
        scale,
    )
    attended = (summed / totals[..., None]).astype(jnp.bfloat16)
    attended = jnp.transpose(attended, (1, 0, 2)).reshape(columns, rows, local_width)
    mixed = lax.psum_scatter(
        jnp.einsum("crh,hd->crd", attended, w_out, preferred_element_type=jnp.float32).astype(
            jnp.bfloat16
        ),
        "head",
        scatter_dimension=0,
        tiled=True,
    ).astype(jnp.float32)
    context = (values + jnp.transpose(mixed, (1, 0, 2))).astype(jnp.bfloat16)
    padded = with_halo(context, (("tile", 0), ("head", 1)), 1).astype(jnp.float32)
    conv = jnp.zeros((rows, cols_dev, width), jnp.float32)
    for i in range(3):
        for j in range(3):
            conv = conv + padded[i : i + rows, j : j + cols_dev] * dw_weight[i, j]
    hidden = jax.nn.gelu(conv + join_bias).astype(jnp.bfloat16)
    projected_out = jnp.einsum("rcd,de->rce", hidden, w_join, preferred_element_type=jnp.float32)
    return (context.astype(jnp.float32) + projected_out).astype(jnp.bfloat16)


def solution(mesh):
    placed = (P("tile", "head", None), P(), P(None, None, "head"), P("head", None), P(), P(), P())
    return jax.shard_map(
        per_device, mesh=mesh, in_specs=placed, out_specs=P("tile", "head", None), check_vma=False
    )
```

profile of v0, /device:TPU:1, one launch (start us, length us, event | category | flops | bytes accessed | tf_op | source)
XLA Modules:
  0.0 259.8 jit_solution(10153033517805802378)
XLA Ops:
  8.3 117.7 %all-gather.4.cloned.1.call-done = bf16[3,1024,1024]{2,1,0:T(8,128)(2,1)} async-done(((bf16[3,1024,256]{2,1,0:T(8,128)(2,1)}), bf16[3,1024,1024]{2,1,0:T(8,128)(2,1)}) %all-gather.4.cloned.1.call-update) | async-done | bytes 6291472 | tf_op jit(solution)/shard_map/all_gather | solution.py:69
  126.0 4.1 %fusion.11 = bf16[3,32,2,1024]{3,1,0,2:T(8,128)(2,1)S(1)} fusion(bf16[3,1024,1024]{2,1,0:T(8,128)(2,1)} %all-gather.4.cloned.1.call-done, bf16[2,32,1024]{2,1,0:T(8,128)(2,1)} %param.7, f32[1024]{0:T(1024)} %param.8, f32[2,32]{1,0:T(2,128)S(1)} %add_rsqrt_fusion), kind=kOutput, calls=%fused_computation.11 | convolution fusion | flops 403111936 | bytes 6820096 | tf_op jit(solution)/shard_map/rcd,jde->jcre/dot_general | solution.py:66
  130.2 3.0 %copy.23 = bf16[3,32,2,1024]{1,2,0,3:T(2,128)(2,1)} copy(bf16[3,32,2,1024]{3,1,0,2:T(8,128)(2,1)S(1)} %fusion.11) | data formatting | bytes 786432 | tf_op jit(solution)/shard_map/convert_element_type | solution.py:71
  133.2 2.6 %reshape.39 = bf16[4,2,24576]{2,1,0:T(2,128)(2,1)S(1)} reshape(bf16[1024,3,2,32]{3,2,1,0:T(2,128)(2,1)} %bitcast.58) | data formatting | bytes 786432
  135.8 13.6 %all_to_all.15 = bf16[4,2,24576]{2,1,0:T(2,128)(2,1)S(1)} all-to-all(bf16[4,2,24576]{2,1,0:T(2,128)(2,1)S(1)} %reshape.39), channel_id=1, replica_groups=mesh['tile'=8,'head'=4] {'head'}, dimensions={0} | all-to-all | bytes 786432 | tf_op jit(solution)/shard_map/all_to_all | solution.py:72
  149.4 1.7 reshape.40
  151.1 3.8 %copy.24 = bf16[3,32,2,4,256]{4,2,1,3,0:T(2,128)(2,1)S(1)} copy(bf16[3,32,2,4,256]{1,2,0,4,3:T(2,128)(2,1)} %bitcast.59) | data formatting | bytes 786432 | tf_op jit(solution)/shard_map/all_to_all | solution.py:72
  157.0 22.9 %all-gather.6.cloned.1.call-done = bf16[2048,256]{1,0:T(8,128)(2,1)} async-done(((bf16[256,256]{1,0:T(8,128)(2,1)}), bf16[2048,256]{1,0:T(8,128)(2,1)}) %all-gather.6.cloned.1.call-update) | async-done | bytes 1048592 | tf_op jit(solution)/shard_map/all_gather | solution.py:83
  179.8 1.5 copy.25
  181.3 1.3 multiply_reduce_fusion
  182.7 3.2 %copy-done.1 = f32[4,256,2048]{2,1,0:T(8,128)} copy-done((f32[4,256,2048]{2,1,0:T(8,128)}, f32[4,256,2048]{2,1,0:T(8,128)S(1)}, u32[]{:S(2)}) %copy-start.1) | copy-done | bytes 8388632
  185.9 1.6 fusion
  187.6 17.7 %all-gather.8.cloned.1.call-done = bf16[2048,256]{1,0:T(8,128)(2,1)} async-done(((bf16[256,256]{1,0:T(8,128)(2,1)}), bf16[2048,256]{1,0:T(8,128)(2,1)}) %all-gather.8.cloned.1.call-update) | async-done | bytes 1048592 | tf_op jit(solution)/shard_map/all_gather | solution.py:84
  205.3 1.5 copy.27
  206.8 5.0 %fusion.29 = bf16[256,4,64]{0,2,1:T(8,128)(2,1)S(1)} fusion(bf16[2048,4,64]{0,2,1:T(8,128)(2,1)S(1)} %bitcast.61, f32[4,256,2048]{2,1,0:T(8,128)} %copy-done.1, f32[4,256]{1,0:T(4,128)S(1)} %get-tuple-element.43, f32[256,4]{0,1:T(4,128)S(1)} %bitcast_add_fusion, f32[256,4]{0,1:T(4,128)S(1)} %get-tuple-element.42), kind=kOutput, calls=%fused_computation.17 | convolution fusion | flops 274923520 | bytes 9580544 | tf_op jit(solution)/shard_map/while/body/eval_jaxpr/hqk,khe->hqe/dot_general | solution.py:41
  212.2 2.1 convolution_convert_fusion
  214.3 19.6 %reduce-scatter.2.cloned.1.call-done = bf16[32,2,1024]{2,0,1:T(8,128)(2,1)} async-done(((bf16[128,2,1024]{2,0,1:T(8,128)(2,1)}), bf16[32,2,1024]{2,0,1:T(8,128)(2,1)}) %reduce-scatter.2.cloned.1.call-update) | async-done | bytes 131088 | tf_op jit(solution)/shard_map/reduce_scatter | solution.py:95
  234.9 5.4 %collective-permute-start = (bf16[1,32,1024]{2,1,0:T(8,128)(2,1)S(1)}, bf16[1,32,1024]{2,1,0:T(8,128)(2,1)S(1)}, u32[]{:S(2)}, u32[]{:S(2)}) collective-permute-start(bf16[1,32,1024]{2,1,0:T(8,128)(2,1)S(1)} %get-tuple-element.30), channel_id=1, source_target_pairs={{0,4},{4,8},{8,12},{12,16},{16,20},{20,24},{24,28},{1,5},{5,9},{9,... | collective-permute-start | bytes 196616 | tf_op jit(solution)/shard_map/ppermute | solution.py:18
  240.3 1.9 collective-permute-start.1
  242.3 3.6 %collective-permute-done.1 = bf16[1,32,1024]{2,1,0:T(8,128)(2,1)S(1)} collective-permute-done((bf16[1,32,1024]{2,1,0:T(8,128)(2,1)S(1)}, bf16[1,32,1024]{2,1,0:T(8,128)(2,1)S(1)}, u32[]{:S(2)}, u32[]{:S(2)}) %collective-permute-start.1) | collective-permute-done | bytes 65568 | tf_op jit(solution)/shard_map/ppermute | solution.py:19
  246.0 1.3 collective-permute-start.2
  247.3 1.3 collective-permute-start.3
  248.6 3.1 %collective-permute-done.3 = bf16[4,1,1024]{2,1,0:T(2,128)(2,1)S(1)} collective-permute-done((bf16[4,1,1024]{2,1,0:T(2,128)(2,1)S(1)}, bf16[4,1,1024]{2,1,0:T(2,128)(2,1)S(1)}, u32[]{:S(2)}, u32[]{:S(2)}) %collective-permute-start.3) | collective-permute-done | bytes 8224 | tf_op jit(solution)/shard_map/ppermute | solution.py:19
  251.9 1.4 fusion.23
  (34 shorter events, 5.4 us)
Async XLA Ops:
  6.5 245.3 %copy-start = (bf16[1024,1024]{1,0:T(8,128)(2,1)S(1)}, bf16[1024,1024]{1,0:T(8,128)(2,1)}, u32[]{:S(2)}) copy-start(bf16[1024,1024]{1,0:T(8,128)(2,1)} %param.13) | copy-start | bytes 6291460
  6.5 119.5 %all-gather.4.cloned.1.call-start = ((), (), s32[]{:S(2)}) async-start(), calls=%async_computation.2 | async-start | bytes 7864320 | tf_op jit(solution)/shard_map/all_gather | solution.py:69
  7.3 172.6 %all-gather.6.cloned.1.call-start = ((), (), s32[]{:S(2)}) async-start(), calls=%async_computation.3 | async-start | bytes 1179648 | tf_op jit(solution)/shard_map/all_gather | solution.py:83
  155.9 49.3 %all-gather.8.cloned.1.call-start = ((), (), s32[]{:S(2)}) async-start(), calls=%async_computation.4 | async-start | bytes 1179648 | tf_op jit(solution)/shard_map/all_gather | solution.py:84
  156.7 77.2 %reduce-scatter.2.cloned.1.call-start = ((), (), s32[]{:S(2)}) async-start(), calls=%async_computation.5 | async-start | bytes 655360 | tf_op jit(solution)/shard_map/reduce_scatter | solution.py:95
  182.6 3.2 %copy-start.1 = (f32[4,256,2048]{2,1,0:T(8,128)}, f32[4,256,2048]{2,1,0:T(8,128)S(1)}, u32[]{:S(2)}) copy-start(f32[4,256,2048]{2,1,0:T(8,128)S(1)} %get-tuple-element.45) | copy-start | bytes 25165828
  187.5 46.4 %copy-start.2 = (bf16[2,32,1024]{2,1,0:T(8,128)(2,1)S(1)}, bf16[2,32,1024]{2,1,0:T(8,128)(2,1)}, u32[]{:S(2)}) copy-start(bf16[2,32,1024]{2,1,0:T(8,128)(2,1)} %param.7) | copy-start | bytes 393220
  187.5 61.0 %copy-start.3 = (f32[3,3,1024]{2,1,0:T(4,128)S(1)}, f32[3,3,1024]{2,1,0:T(4,128)}, u32[]{:S(2)}) copy-start(f32[3,3,1024]{2,1,0:T(4,128)} %param.11) | copy-start | bytes 110596
  187.5 64.3 %copy-start.4 = (f32[1024]{0:T(1024)S(1)}, f32[1024]{0:T(1024)}, u32[]{:S(2)}) copy-start(f32[1024]{0:T(1024)} %param.12) | copy-start | bytes 12292
  234.9 7.4 %collective-permute-start = (bf16[1,32,1024]{2,1,0:T(8,128)(2,1)S(1)}, bf16[1,32,1024]{2,1,0:T(8,128)(2,1)S(1)}, u32[]{:S(2)}, u32[]{:S(2)}) collective-permute-start(bf16[1,32,1024]{2,1,0:T(8,128)(2,1)S(1)} %get-tuple-element.30), channel_id=1, source_target_pairs={{0,4},{4,8},{8,12},{12,16},{16,20},{20,24},{24,28},{1,5},{5,9},{9,... | collective-permute-start | bytes 196616 | tf_op jit(solution)/shard_map/ppermute | solution.py:18
  240.3 5.6 %collective-permute-start.1 = (bf16[1,32,1024]{2,1,0:T(8,128)(2,1)S(1)}, bf16[1,32,1024]{2,1,0:T(8,128)(2,1)S(1)}, u32[]{:S(2)}, u32[]{:S(2)}) collective-permute-start(bf16[1,32,1024]{2,1,0:T(8,128)(2,1)S(1)} %get-tuple-element.32), channel_id=1, source_target_pairs={{4,0},{8,4},{12,8},{16,12},{20,16},{24,20},{28,24},{5,1},{9,5},{13... | collective-permute-start | bytes 196616 | tf_op jit(solution)/shard_map/ppermute | solution.py:19
  246.0 2.6 %collective-permute-start.2 = (bf16[4,1,1024]{2,1,0:T(2,128)(2,1)S(1)}, bf16[4,1,1024]{2,1,0:T(2,128)(2,1)S(1)}, u32[]{:S(2)}, u32[]{:S(2)}) collective-permute-start(bf16[4,1,1024]{2,1,0:T(2,128)(2,1)S(1)} %get-tuple-element.20), channel_id=1, source_target_pairs={{0,1},{1,2},{2,3},{4,5},{5,6},{6,7},{8,9},{9,10},{10,11},{12,13},{... | collective-permute-start | bytes 24584 | tf_op jit(solution)/shard_map/ppermute | solution.py:18
  247.3 4.5 %collective-permute-start.3 = (bf16[4,1,1024]{2,1,0:T(2,128)(2,1)S(1)}, bf16[4,1,1024]{2,1,0:T(2,128)(2,1)S(1)}, u32[]{:S(2)}, u32[]{:S(2)}) collective-permute-start(bf16[4,1,1024]{2,1,0:T(2,128)(2,1)S(1)} %get-tuple-element.28), channel_id=1, source_target_pairs={{1,0},{2,1},{3,2},{5,4},{6,5},{7,6},{9,8},{10,9},{11,10},{13,12},{... | collective-permute-start | bytes 24584 | tf_op jit(solution)/shard_map/ppermute | solution.py:19
Sparse Core Ops, SparseCore 0:
  8.9 117.0 all-gather.3
  156.1 23.7 all-gather.5
  181.7 23.4 all-gather.7
  214.5 19.4 reduce-scatter.1
where the time goes:
time: 260 us
  waiting for transfers between devices  185 us (71%)
  local copies, waits for them, and re-layouts  19.6 us (8%)
  matrix products  14 us (5%)
  blocking collectives  13.6 us (5%)
  between operations  13.3 us (5%)
  starting transfers between devices  10.1 us (4%)
  other arithmetic  3.75 us (1%)
    all_gather x1, waiting for transfers between devices, per_device(): lax.all_gather(w_qkv, 'head', axis=2, tiled=True)  118 us
    all_gather x1, waiting for transfers between devices, per_device(): key_piece = lax.all_gather(keys, 'tile', axis=0, tiled=True)  22.9 us
    reduce_scatter x1, waiting for transfers between devices, per_device(): lax.psum_scatter(jnp.einsum('crh,hd->crd', attended, w_out, preferred_ele...  19.6 us
    all_gather x1, waiting for transfers between devices, per_device(): value_piece = lax.all_gather(vals, 'tile', axis=0, tiled=True)  17.7 us
    all_to_all x1, blocking collectives, per_device(): lax.all_to_all(all_heads, 'head', split_axis=3, concat_axis=1, tiled=True)  13.6 us
    unnamed x12, local copies, waits for them, and re-layouts  7.52 us
    ppermute x2, waiting for transfers between devices, with_halo(): after = lax.ppermute(leading, axis, down)  6.77 us
    ppermute x2, starting transfers between devices, with_halo(): before = lax.ppermute(last, axis, up)  6.72 us
  transfers between devices with their start and end apart: 8, of which 6 were waited for; matrix products, arithmetic and copies ran while one was open for 2% of the time, Pallas kernels for 0%

commit v1 on v0

--- a/solution.py
+++ b/solution.py
@@ -63,22 +63,20 @@
     normed = (
         values * lax.rsqrt(jnp.mean(values * values, axis=-1, keepdims=True) + 1e-06) * norm_gain
     ).astype(jnp.bfloat16)
-    all_heads = jnp.einsum(
-        "rcd,jde->jcre",
-        normed,
-        lax.all_gather(w_qkv, "head", axis=2, tiled=True),
-        preferred_element_type=jnp.float32,
-    ).astype(jnp.bfloat16)
-    projected = lax.all_to_all(all_heads, "head", split_axis=3, concat_axis=1, tiled=True)
-    columns = projected.shape[1]
-    local_width = projected.shape[3]
+    gathered = lax.all_gather(normed, "head", axis=1, tiled=True)
+    columns = gathered.shape[1]
+    local_width = w_qkv.shape[2]
     head_dim = width // HEADS
     local_heads = local_width // head_dim
     seq_local = columns * rows
     scale = 1.0 / head_dim**0.5
+    tokens = jnp.transpose(gathered, (1, 0, 2)).reshape(seq_local, width)
+    projected = jnp.einsum(
+        "td,jde->jte", tokens, w_qkv, preferred_element_type=jnp.float32
+    ).astype(jnp.bfloat16)
     queries = projected[0].reshape(seq_local, local_heads, head_dim)
-    keys = projected[1].reshape(seq_local, local_width)
-    vals = projected[2].reshape(seq_local, local_width)
+    keys = projected[1]
+    vals = projected[2]
     start_state = empty_state(local_heads, seq_local, head_dim)
     key_piece = lax.all_gather(keys, "tile", axis=0, tiled=True)
     value_piece = lax.all_gather(vals, "tile", axis=0, tiled=True)

time: 260 us -> 133 us (0.51)
  waiting for transfers between devices: 185 us -> 71.7 us
  local copies, waits for them, and re-layouts: 19.6 us -> 5.13 us
    all_gather x1 -> x0, waiting for transfers between devices: 118 us -> none  [per_device(): lax.all_gather(w_qkv, 'head', axis=2, tiled=True)]
    all_gather x0 -> x1, blocking collectives: none -> 15.3 us  [per_device(): gathered = lax.all_gather(normed, 'head', axis=1, tiled=True)]
    all_to_all x1 -> x0, blocking collectives: 13.6 us -> none  [per_device(): lax.all_to_all(all_heads, 'head', split_axis=3, concat_axis=1, tiled=True)]
    unnamed x12, local copies, waits for them, and re-layouts: 7.52 us -> 3.24 us
    all_to_all x1 -> x0, local copies, waits for them, and re-layouts: 3.75 us -> none  [per_device(): lax.all_to_all(all_heads, 'head', split_axis=3, concat_axis=1, tiled=True)]
    all_gather x1, waiting for transfers between devices: 22.9 us -> 26.6 us  [per_device(): key_piece = lax.all_gather(keys, 'tile', axis=0, tiled=True)]
    convert_element_type x1 -> x0, local copies, waits for them, and re-layouts: 2.99 us -> none  [per_device(): all_heads = jnp.einsum('rcd,jde->jcre', normed, lax.all_gather(w_qkv, 'he...]
    all_gather x2 -> x0, local copies, waits for them, and re-layouts: 2.96 us -> none  [the longest x1 1.48 us: per_device(): key_piece = lax.all_gather(keys, 'tile', axis=0, tiled=True)]
  transfers between devices with their start and end apart: 8 -> 7, of which waited for: 6 -> 5; matrix products, arithmetic and copies ran while one was open for 2% -> 3% of each run, Pallas kernels for 0% -> 0%
where the time goes in v1:
time: 133 us
  waiting for transfers between devices  71.7 us (54%)
  blocking collectives  15.3 us (12%)
  between operations  13.3 us (10%)
  matrix products  12.5 us (9%)
  starting transfers between devices  9.97 us (7%)
  local copies, waits for them, and re-layouts  5.13 us (4%)
  other arithmetic  4.91 us (4%)
    all_gather x1, waiting for transfers between devices, per_device(): key_piece = lax.all_gather(keys, 'tile', axis=0, tiled=True)  26.6 us
    reduce_scatter x1, waiting for transfers between devices, per_device(): lax.psum_scatter(jnp.einsum('crh,hd->crd', attended, w_out, preferred_ele...  19.6 us
    all_gather x1, waiting for transfers between devices, per_device(): value_piece = lax.all_gather(vals, 'tile', axis=0, tiled=True)  18 us
    all_gather x1, blocking collectives, per_device(): gathered = lax.all_gather(normed, 'head', axis=1, tiled=True)  15.3 us
    ppermute x2, waiting for transfers between devices, with_halo(): after = lax.ppermute(leading, axis, down)  6.77 us
    ppermute x2, starting transfers between devices, with_halo(): before = lax.ppermute(last, axis, up)  6.68 us
    dot_general x1, matrix products, one_block(): jnp.einsum('hqk,khe->hqe', weights.astype(jnp.bfloat16), value_block, pre...  5.24 us
    unnamed x12, local copies, waits for them, and re-layouts  3.24 us
  transfers between devices with their start and end apart: 7, of which 5 were waited for; matrix products, arithmetic and copies ran while one was open for 3% of the time, Pallas kernels for 0%

profile of v1, /device:TPU:1, one launch (start us, length us, event | category | flops | bytes accessed | tf_op | source)
XLA Modules:
  0.0 132.7 jit_solution(16049080055621691610)
XLA Ops:
  6.5 1.2 fusion.26
  7.7 1.0 fusion.28
  8.7 15.3 %all_gather.9 = bf16[2,128,1024]{2,1,0:T(8,128)(2,1)S(1)} all-gather(bf16[2,32,1024]{2,1,0:T(8,128)(2,1)S(1)} %fusion.28), channel_id=1, replica_groups=mesh['tile'=8,'head'=4] {'head'}, dimensions={1}, use_global_device_ids=true | all-gather | bytes 655360 | tf_op jit(solution)/shard_map/all_gather | solution.py:66
  24.0 0.5 copy.11
  24.8 2.1 %fusion.6 = bf16[3,256,256]{1,2,0:T(8,128)(2,1)S(1)} fusion(bf16[256,1024,1]{1,0,2:T(8,128)(2,1)S(1)} %reshape.37, bf16[3,1024,256]{2,1,0:T(8,128)(2,1)} %param.9), kind=kOutput, calls=%fused_computation.9 | convolution fusion | flops 402849792 | bytes 2490368 | tf_op jit(solution)/shard_map/td,jde->jte/dot_general | solution.py:74
  26.9 0.7 fusion.68
  27.7 0.7 all-gather.7.cloned.1.call-update
  28.5 26.6 %all-gather.5.cloned.1.call-done = bf16[1,2048,256]{1,2,0:T(8,128)(2,1)} async-done(((bf16[1,256,256]{1,2,0:T(8,128)(2,1)}), bf16[1,2048,256]{1,2,0:T(8,128)(2,1)}) %all-gather.5.cloned.1.call-update) | async-done | bytes 1048592 | tf_op jit(solution)/shard_map/all_gather | solution.py:81
  55.0 2.6 %multiply_reduce_fusion = (f32[4,256]{1,0:T(4,128)S(1)}, f32[4,256,2048]{2,1,0:T(8,128)S(1)}) fusion(bf16[256,4,64]{0,2,1:T(8,128)(2,1)S(1)} %bitcast.48, bf16[2048,4,64]{0,2,1:T(8,128)(2,1)} %bitcast.47), kind=kOutput, calls=%fused_computation.1 | convolution fusion | flops 272628736 | bytes 9572352 | tf_op jit(solution)/shard_map/while/body/eval_jaxpr/qhe,khe->hqk/dot_general | solution.py:34
  57.6 3.2 %copy-done.1 = f32[4,256,2048]{2,1,0:T(8,128)} copy-done((f32[4,256,2048]{2,1,0:T(8,128)}, f32[4,256,2048]{2,1,0:T(8,128)S(1)}, u32[]{:S(2)}) %copy-start.1) | copy-done | bytes 8388632
  60.8 1.6 %fusion = f32[4,256]{1,0:T(4,128)S(1)} fusion(f32[4,256,2048]{2,1,0:T(8,128)S(1)} %get-tuple-element.45, f32[4,256]{1,0:T(4,128)S(1)} %get-tuple-element.43), kind=kLoop, calls=%fused_computation.2 | loop fusion | flops 6290432 | bytes 8396800 | tf_op jit(solution)/shard_map/while/body/eval_jaxpr/reduce_sum | solution.py:40
  62.5 18.0 %all-gather.7.cloned.1.call-done = bf16[1,2048,256]{1,2,0:T(8,128)(2,1)} async-done(((bf16[1,256,256]{1,2,0:T(8,128)(2,1)}), bf16[1,2048,256]{1,2,0:T(8,128)(2,1)}) %all-gather.7.cloned.1.call-update) | async-done | bytes 1048592 | tf_op jit(solution)/shard_map/all_gather | solution.py:82
  80.5 5.2 %fusion.22 = bf16[256,4,64]{0,2,1:T(8,128)(2,1)S(1)} fusion(bf16[2048,4,64]{0,2,1:T(8,128)(2,1)} %bitcast.58, f32[4,256,2048]{2,1,0:T(8,128)} %copy-done.1, f32[4,256]{1,0:T(4,128)S(1)} %get-tuple-element.43, f32[256,4]{0,1:T(4,128)S(1)} %bitcast_add_fusion, f32[256,4]{0,1:T(4,128)S(1)} %get-tuple-element.42), kind=kOutput, calls=%fused_computation.15 | convolution fusion | flops 274923520 | bytes 9580544 | tf_op jit(solution)/shard_map/while/body/eval_jaxpr/hqk,khe->hqe/dot_general | solution.py:41
  85.9 0.2 reshape.32
  86.2 1.1 convolution_convert_fusion
  87.3 19.6 %reduce-scatter.2.cloned.1.call-done = bf16[32,2,1024]{2,0,1:T(8,128)(2,1)} async-done(((bf16[128,2,1024]{2,0,1:T(8,128)(2,1)}), bf16[32,2,1024]{2,0,1:T(8,128)(2,1)}) %reduce-scatter.2.cloned.1.call-update) | async-done | bytes 131088 | tf_op jit(solution)/shard_map/reduce_scatter | solution.py:93
  106.9 0.9 fusion.29
  107.9 5.4 %collective-permute-start = (bf16[1,32,1024]{2,1,0:T(8,128)(2,1)S(1)}, bf16[1,32,1024]{2,1,0:T(8,128)(2,1)S(1)}, u32[]{:S(2)}, u32[]{:S(2)}) collective-permute-start(bf16[1,32,1024]{2,1,0:T(8,128)(2,1)S(1)} %get-tuple-element.30), channel_id=1, source_target_pairs={{0,4},{4,8},{8,12},{12,16},{16,20},{20,24},{24,28},{1,5},{5,9},{9,... | collective-permute-start | bytes 196616 | tf_op jit(solution)/shard_map/ppermute | solution.py:18
  113.3 1.9 %collective-permute-start.1 = (bf16[1,32,1024]{2,1,0:T(8,128)(2,1)S(1)}, bf16[1,32,1024]{2,1,0:T(8,128)(2,1)S(1)}, u32[]{:S(2)}, u32[]{:S(2)}) collective-permute-start(bf16[1,32,1024]{2,1,0:T(8,128)(2,1)S(1)} %get-tuple-element.32), channel_id=1, source_target_pairs={{4,0},{8,4},{12,8},{16,12},{20,16},{24,20},{28,24},{5,1},{9,5},{13... | collective-permute-start | bytes 196616 | tf_op jit(solution)/shard_map/ppermute | solution.py:19
  115.2 3.6 %collective-permute-done.1 = bf16[1,32,1024]{2,1,0:T(8,128)(2,1)S(1)} collective-permute-done((bf16[1,32,1024]{2,1,0:T(8,128)(2,1)S(1)}, bf16[1,32,1024]{2,1,0:T(8,128)(2,1)S(1)}, u32[]{:S(2)}, u32[]{:S(2)}) %collective-permute-start.1) | collective-permute-done | bytes 65568 | tf_op jit(solution)/shard_map/ppermute | solution.py:19
  118.9 1.3 collective-permute-start.2
  120.2 1.3 collective-permute-start.3
  121.5 3.1 %collective-permute-done.3 = bf16[4,1,1024]{2,1,0:T(2,128)(2,1)S(1)} collective-permute-done((bf16[4,1,1024]{2,1,0:T(2,128)(2,1)S(1)}, bf16[4,1,1024]{2,1,0:T(2,128)(2,1)S(1)}, u32[]{:S(2)}, u32[]{:S(2)}) %collective-permute-start.3) | collective-permute-done | bytes 8224 | tf_op jit(solution)/shard_map/ppermute | solution.py:19
  124.8 1.4 %fusion.16 = bf16[2,32,1024]{2,1,0:T(8,128)(2,1)} fusion(bf16[1024,1024]{1,0:T(8,128)(2,1)S(1)} %copy-done, bf16[2,32,1024]{2,1,0:T(8,128)(2,1)S(1)} %fusion.29, f32[4,34,1024]{2,1,0:T(8,128)S(1)} %maximum_convert_fusion, f32[1024]{0:T(1024)S(1)} %copy-done.5, f32[1024]{0:T(1024)S(1)} %bitcast.56, f32[1024]{0:T(1024)S(1)} %bitcast.57, ...), kind=kOutput, calls=%fused_computation.13 | convolution fusion | flops 136183808 | bytes 4759552 | tf_op jit(solution)/shard_map/rcd,de->rce/dot_general | solution.py:108
  (27 shorter events, 0.7 us)
Async XLA Ops:
  6.5 118.3 %copy-start = (bf16[1024,1024]{1,0:T(8,128)(2,1)S(1)}, bf16[1024,1024]{1,0:T(8,128)(2,1)}, u32[]{:S(2)}) copy-start(bf16[1024,1024]{1,0:T(8,128)(2,1)} %param.13) | copy-start | bytes 6291460
  6.5 48.5 %all-gather.5.cloned.1.call-start = ((), (), s32[]{:S(2)}) async-start(), calls=%async_computation.2 | async-start | bytes 1179648 | tf_op jit(solution)/shard_map/all_gather | solution.py:81
  27.7 52.8 %all-gather.7.cloned.1.call-start = ((), (), s32[]{:S(2)}) async-start(), calls=%async_computation.3 | async-start | bytes 1179648 | tf_op jit(solution)/shard_map/all_gather | solution.py:82
  28.4 78.5 %reduce-scatter.2.cloned.1.call-start = ((), (), s32[]{:S(2)}) async-start(), calls=%async_computation.1 | async-start | bytes 655360 | tf_op jit(solution)/shard_map/reduce_scatter | solution.py:93
  57.6 3.2 %copy-start.1 = (f32[4,256,2048]{2,1,0:T(8,128)}, f32[4,256,2048]{2,1,0:T(8,128)S(1)}, u32[]{:S(2)}) copy-start(f32[4,256,2048]{2,1,0:T(8,128)S(1)} %get-tuple-element.45) | copy-start | bytes 25165828
  60.8 25.3 %copy-start.3 = (bf16[256,1024]{1,0:T(8,128)(2,1)S(1)}, bf16[256,1024]{1,0:T(8,128)(2,1)}, u32[]{:S(2)}) copy-start(bf16[256,1024]{1,0:T(8,128)(2,1)} %param.10) | copy-start | bytes 1572868
  62.5 44.4 %copy-start.2 = (bf16[2,32,1024]{2,1,0:T(8,128)(2,1)S(1)}, bf16[2,32,1024]{2,1,0:T(8,128)(2,1)}, u32[]{:S(2)}) copy-start(bf16[2,32,1024]{2,1,0:T(8,128)(2,1)} %param.7) | copy-start | bytes 393220
  62.5 59.0 %copy-start.4 = (f32[3,3,1024]{2,1,0:T(4,128)S(1)}, f32[3,3,1024]{2,1,0:T(4,128)}, u32[]{:S(2)}) copy-start(f32[3,3,1024]{2,1,0:T(4,128)} %param.11) | copy-start | bytes 110596
  62.5 62.3 %copy-start.5 = (f32[1024]{0:T(1024)S(1)}, f32[1024]{0:T(1024)}, u32[]{:S(2)}) copy-start(f32[1024]{0:T(1024)} %param.12) | copy-start | bytes 12292
  107.9 7.3 %collective-permute-start = (bf16[1,32,1024]{2,1,0:T(8,128)(2,1)S(1)}, bf16[1,32,1024]{2,1,0:T(8,128)(2,1)S(1)}, u32[]{:S(2)}, u32[]{:S(2)}) collective-permute-start(bf16[1,32,1024]{2,1,0:T(8,128)(2,1)S(1)} %get-tuple-element.30), channel_id=1, source_target_pairs={{0,4},{4,8},{8,12},{12,16},{16,20},{20,24},{24,28},{1,5},{5,9},{9,... | collective-permute-start | bytes 196616 | tf_op jit(solution)/shard_map/ppermute | solution.py:18
  113.3 5.6 %collective-permute-start.1 = (bf16[1,32,1024]{2,1,0:T(8,128)(2,1)S(1)}, bf16[1,32,1024]{2,1,0:T(8,128)(2,1)S(1)}, u32[]{:S(2)}, u32[]{:S(2)}) collective-permute-start(bf16[1,32,1024]{2,1,0:T(8,128)(2,1)S(1)} %get-tuple-element.32), channel_id=1, source_target_pairs={{4,0},{8,4},{12,8},{16,12},{20,16},{24,20},{28,24},{5,1},{9,5},{13... | collective-permute-start | bytes 196616 | tf_op jit(solution)/shard_map/ppermute | solution.py:19
  118.9 2.6 %collective-permute-start.2 = (bf16[4,1,1024]{2,1,0:T(2,128)(2,1)S(1)}, bf16[4,1,1024]{2,1,0:T(2,128)(2,1)S(1)}, u32[]{:S(2)}, u32[]{:S(2)}) collective-permute-start(bf16[4,1,1024]{2,1,0:T(2,128)(2,1)S(1)} %get-tuple-element.20), channel_id=1, source_target_pairs={{0,1},{1,2},{2,3},{4,5},{5,6},{6,7},{8,9},{9,10},{10,11},{12,13},{... | collective-permute-start | bytes 24584 | tf_op jit(solution)/shard_map/ppermute | solution.py:18
  120.2 4.5 %collective-permute-start.3 = (bf16[4,1,1024]{2,1,0:T(2,128)(2,1)S(1)}, bf16[4,1,1024]{2,1,0:T(2,128)(2,1)S(1)}, u32[]{:S(2)}, u32[]{:S(2)}) collective-permute-start(bf16[4,1,1024]{2,1,0:T(2,128)(2,1)S(1)} %get-tuple-element.28), channel_id=1, source_target_pairs={{1,0},{2,1},{3,2},{5,4},{6,5},{7,6},{9,8},{10,9},{11,10},{13,12},{... | collective-permute-start | bytes 24584 | tf_op jit(solution)/shard_map/ppermute | solution.py:19
Sparse Core Ops, SparseCore 0:
  27.8 27.1 all-gather.4
  56.9 23.5 all-gather.6
  87.4 19.4 reduce-scatter.1

commit v2 on v1

--- a/solution.py
+++ b/solution.py
@@ -1,8 +1,11 @@
+import functools
 import math
 
 import jax
 import jax.numpy as jnp
 from jax import lax
+from jax.experimental import pallas as pl
+from jax.experimental.pallas import tpu as pltpu
 from jax.sharding import PartitionSpec as P
 
 HEADS = 16
@@ -109,8 +112,377 @@
     return (context.astype(jnp.float32) + projected_out).astype(jnp.bfloat16)
 
 
+MESH = pl.DeviceIdType.MESH
+
+
+def fused_kernel(
+    tiles,
+    parts,
+    bott_ref,
+    gain_ref,
+    wqkv_hbm,
+    wout_hbm,
+    dw_ref,
+    bias_ref,
+    wjoin_hbm,
+    out_ref,
+    wqkv,
+    wout,
+    wjoin,
+    nrm,
+    snd,
+    rcv,
+    asnd,
+    arcv,
+    psnd,
+    prcv,
+    pad,
+    hrow_s,
+    hcol_s,
+    hrow,
+    hcol,
+    wsem,
+    nsend,
+    nrecv,
+    qsend,
+    qrecv,
+    asend,
+    arecv,
+    psend,
+    precv,
+    hsend,
+    hrecv,
+):
+    f32, bf16 = jnp.float32, jnp.bfloat16
+    t = lax.axis_index("tile")
+    z = lax.axis_index("head")
+    rows, cols, width = bott_ref.shape
+    tok = rows * cols
+    local = wqkv.shape[2]
+    heads = tiles // parts
+    head_dim = local // heads
+    qpart = tok // parts
+    z0, z1 = lax.rem(z, 2), z // 2
+
+    def zpeer(k):
+        return lax.rem(z0 + k % 2, 2) + 2 * lax.rem(z1 + k // 2, 2)
+
+    zleft, zright = lax.rem(z + 3, 4), lax.rem(z + 1, 4)
+    tup, tdown = lax.rem(t + tiles - 1, tiles), lax.rem(t + 1, tiles)
+
+    loads = [
+        pltpu.make_async_copy(wqkv_hbm, wqkv, wsem.at[0]),
+        pltpu.make_async_copy(wout_hbm, wout, wsem.at[1]),
+        pltpu.make_async_copy(wjoin_hbm, wjoin, wsem.at[2]),
+    ]
+    for load in loads:
+        load.start()
+
+    barrier = pltpu.get_barrier_semaphore()
+    for k in range(1, 4):
+        pl.semaphore_signal(barrier, inc=1, device_id=(t, zpeer(k)), device_id_type=MESH)
+
+    @pl.loop(1, tiles)
+    def _(p):
+        pl.semaphore_signal(
+            barrier, inc=1, device_id=(lax.rem(t + p, tiles), z), device_id_type=MESH
+        )
+
+    for dt in (tup, tdown):
+        for dz in (zleft, zright):
+            pl.semaphore_signal(barrier, inc=1, device_id=(dt, dz), device_id_type=MESH)
+
+    values = bott_ref[...].reshape(tok, width).astype(f32)
+    mean = jnp.mean(values * values, axis=-1, keepdims=True)
+    nrm[0] = (values * lax.rsqrt(mean + 1e-06) * gain_ref[...]).astype(bf16)
+    pad[...] = jnp.zeros_like(pad)
+
+    pl.semaphore_wait(barrier, 3 + (tiles - 1) + 4)
+
+    ncopies = []
+    for k in (1, 2, 3):
+        copy = pltpu.make_async_remote_copy(
+            src_ref=nrm.at[0],
+            dst_ref=nrm.at[k],
+            send_sem=nsend.at[k - 1],
+            recv_sem=nrecv.at[k - 1],
+            device_id=(t, zpeer(k)),
+            device_id_type=MESH,
+        )
+        copy.start()
+        ncopies.append(copy)
+    loads[0].wait()
+
+    low = lax.broadcasted_iota(jnp.int32, (tok, 2 * head_dim), 1) < head_dim
+    zero = jnp.zeros((tok, 2 * head_dim), f32)
+    lanes = 2 * head_dim
+    scale = 1.0 / head_dim**0.5
+
+    def all_of(ref, sem):
+        pltpu.make_async_copy(ref, ref, sem).wait()
+
+    for k in range(4):
+        if k > 0:
+            ncopies[k - 1].wait_recv()
+        x = nrm[k]
+        q = jnp.dot(x, wqkv[0], preferred_element_type=f32) * scale
+        key = jnp.dot(x, wqkv[1], preferred_element_type=f32)
+        val = jnp.dot(x, wqkv[2], preferred_element_type=f32)
+        for pair in range(heads // 2):
+            cut = slice(pair * lanes, (pair + 1) * lanes)
+            v2 = val[:, cut]
+            k2 = pltpu.roll(key[:, cut], head_dim, 1)
+            q2 = pltpu.roll(q[:, cut], head_dim, 1)
+            even = jnp.where(low, v2, k2).astype(bf16)
+            odd = jnp.where(low, k2, v2).astype(bf16)
+            qeven = jnp.where(low, zero, q2).astype(bf16)
+            qodd = jnp.where(low, q2, zero).astype(bf16)
+            for h, kv, qq in ((2 * pair, even, qeven), (2 * pair + 1, odd, qodd)):
+                for c in range(parts):
+                    d = h * parts + c
+                    snd[k, d, :tok] = kv
+                    snd[k, d, tok:] = qq[c * qpart : (c + 1) * qpart]
+
+        @pl.loop(1, tiles)
+        def _(p):
+            j = lax.rem(t + p, tiles)
+            pltpu.make_async_remote_copy(
+                src_ref=snd.at[k, j],
+                dst_ref=rcv.at[k, t],
+                send_sem=qsend.at[k],
+                recv_sem=qrecv.at[k],
+                device_id=(j, z),
+                device_id_type=MESH,
+            ).start()
+
+        rcv[k, t] = snd[k, t]
+
+    for k in range(4):
+        all_of(rcv.at[k, pl.ds(0, tiles - 1)], qrecv.at[k])
+
+    loads[1].wait()
+    order = (3, 2, 1, 0)
+    kvs = [rcv[k, :, :tok].reshape(tiles * tok, lanes) for k in range(4)]
+    own = [None]
+
+    def project(k):
+        all_of(arcv.at[k, pl.ds(0, tiles - 1)], arecv.at[k])
+        lowb = lax.broadcasted_iota(jnp.int32, (tok, lanes), 1) < head_dim
+        pieces = []
+        for pair in range(heads // 2):
+            first = arcv[k, 2 * pair * parts : (2 * pair + 1) * parts].reshape(tok, lanes)
+            second = arcv[k, (2 * pair + 1) * parts : (2 * pair + 2) * parts].reshape(tok, lanes)
+            pieces.append(jnp.where(lowb, first, second))
+        mixed = jnp.dot(jnp.concatenate(pieces, axis=1), wout[...], preferred_element_type=f32)
+        if k == 0:
+            own[0] = mixed
+            return None
+        psnd[k - 1] = mixed.astype(bf16)
+        copy = pltpu.make_async_remote_copy(
+            src_ref=psnd.at[k - 1],
+            dst_ref=prcv.at[k - 1],
+            send_sem=psend.at[k - 1],
+            recv_sem=precv.at[k - 1],
+            device_id=(t, zpeer(k)),
+            device_id_type=MESH,
+        )
+        copy.start()
+        return copy
+
+    pcopies = []
+    for step, k in enumerate(order):
+        qs = rcv[k, :, tok:].reshape(tiles * qpart, lanes)
+        scores = [
+            lax.dot_general(qs, kv, (((1,), (1,)), ((), ())), preferred_element_type=f32)
+            for kv in kvs
+        ]
+        top = functools.reduce(jnp.maximum, [jnp.max(s, axis=-1, keepdims=True) for s in scores])
+        total, summed = 0.0, 0.0
+        for s, kv in zip(scores, kvs):
+            w = jnp.exp(s - top)
+            total = total + jnp.sum(w, axis=-1, keepdims=True)
+            summed = summed + jnp.dot(w.astype(bf16), kv, preferred_element_type=f32)
+        asnd[k] = (summed / total).astype(bf16).reshape(tiles, qpart, lanes)
+
+        @pl.loop(1, tiles)
+        def _(p):
+            j = lax.rem(t + p, tiles)
+            pltpu.make_async_remote_copy(
+                src_ref=asnd.at[k, j],
+                dst_ref=arcv.at[k, t],
+                send_sem=asend.at[k],
+                recv_sem=arecv.at[k],
+                device_id=(j, z),
+                device_id_type=MESH,
+            ).start()
+
+        arcv[k, t] = asnd[k, t]
+        if step > 0:
+            pcopies.append(project(order[step - 1]))
+    project(order[-1])
+
+    context = bott_ref[...].reshape(tok, width).astype(f32)
+    mixed = own[0]
+    for copy, k in zip(pcopies, order):
+        copy.wait_recv()
+        mixed = mixed + prcv[k - 1].astype(f32)
+    context = (context + mixed).astype(bf16)
+    wide = context.astype(f32).reshape(rows, cols, width)
+    narrow = context.reshape(rows, cols, width)
+    pad[1 : rows + 1, 8 : 8 + cols] = wide
+    hrow_s[0] = narrow[0]
+    hrow_s[1] = narrow[rows - 1]
+    first_row = lax.broadcasted_iota(jnp.int32, (16, width), 0) == 0
+    for side, c in ((0, 0), (1, cols - 1)):
+        hcol_s[side] = jnp.where(
+            first_row, wide[0, c : c + 1], wide[rows - 1, c : c + 1]
+        ).astype(bf16)
+
+    hcopies = []
+    plan = [
+        (hrow_s.at[1], hrow.at[0], (tdown, z)),
+        (hrow_s.at[0], hrow.at[1], (tup, z)),
+        (hcol_s.at[1], hcol.at[0], (t, zright)),
+        (hcol_s.at[0], hcol.at[1], (t, zleft)),
+        (hcol_s.at[1], hcol.at[2], (tdown, zright)),
+        (hcol_s.at[0], hcol.at[3], (tdown, zleft)),
+        (hcol_s.at[1], hcol.at[4], (tup, zright)),
+        (hcol_s.at[0], hcol.at[5], (tup, zleft)),
+    ]
+    for n, (src, dst, target) in enumerate(plan):
+        copy = pltpu.make_async_remote_copy(
+            src_ref=src,
+            dst_ref=dst,
+            send_sem=hsend.at[n],
+            recv_sem=hrecv.at[n],
+            device_id=target,
+            device_id_type=MESH,
+        )
+        copy.start()
+        hcopies.append(copy)
+    loads[2].wait()
+
+    for copy in ncopies:
+        copy.wait_send()
+    for k in range(4):
+        all_of(snd.at[k, pl.ds(0, tiles - 1)], qsend.at[k])
+        all_of(asnd.at[k, pl.ds(0, tiles - 1)], asend.at[k])
+    for copy in pcopies:
+        copy.wait_send()
+
+    for copy in hcopies:
+        copy.wait_recv()
+    up_ok = (t > 0).astype(f32)
+    down_ok = (t < tiles - 1).astype(f32)
+    left_ok = (z > 0).astype(f32)
+    right_ok = (z < 3).astype(f32)
+    end = 8 + cols
+    pad[0, 8:end] = hrow[0].astype(f32) * up_ok
+    pad[rows + 1, 8:end] = hrow[1].astype(f32) * down_ok
+    for n, ok, at in ((0, left_ok, 7), (1, right_ok, end)):
+        column = hcol[n].astype(f32) * ok
+        pad[1, at : at + 1] = column[0:1]
+        pad[2, at : at + 1] = column[1:2]
+        above = hcol[2 + n].astype(f32) * (ok * up_ok)
+        pad[0, at : at + 1] = above[1:2]
+        below = hcol[4 + n].astype(f32) * (ok * down_ok)
+        pad[rows + 1, at : at + 1] = below[0:1]
+
+    total = context.astype(f32)
+    step = 256
+    for c in range(0, width, step):
+        cut = slice(c, c + step)
+        conv = jnp.zeros((rows, cols, step), f32)
+        for i in range(3):
+            for j in range(3):
+                conv = conv + pad[i : i + rows, 7 + j : 7 + j + cols, cut] * dw_ref[i, j : j + 1, cut]
+        hidden = jax.nn.gelu(conv + bias_ref[:, cut]).astype(bf16).reshape(tok, step)
+        total = total + jnp.dot(hidden, wjoin[cut, :], preferred_element_type=f32)
+    out_ref[...] = total.astype(bf16).reshape(rows, cols, width)
+    for copy in hcopies:
+        copy.wait_send()
+
+
+def fused(tiles, parts, bott, norm_gain, w_qkv, w_out, dw_weight, join_bias, w_join):
+    rows, cols, width = bott.shape
+    tok = rows * cols
+    local = w_qkv.shape[2]
+    lanes = 2 * local * parts // tiles
+    qpart = tok // parts
+    bf16 = jnp.bfloat16
+    vmem = pl.BlockSpec(memory_space=pltpu.VMEM)
+    hbm = pl.BlockSpec(memory_space=pl.ANY)
+    dma = pltpu.SemaphoreType.DMA
+    return pl.pallas_call(
+        functools.partial(fused_kernel, tiles, parts),
+        out_shape=jax.ShapeDtypeStruct(bott.shape, bf16),
+        in_specs=[vmem, vmem, hbm, hbm, vmem, vmem, hbm],
+        out_specs=vmem,
+        scratch_shapes=[
+            pltpu.VMEM(w_qkv.shape, bf16),
+            pltpu.VMEM(w_out.shape, bf16),
+            pltpu.VMEM(w_join.shape, bf16),
+            pltpu.VMEM((4, tok, width), bf16),
+            pltpu.VMEM((4, tiles, tok + qpart, lanes), bf16),
+            pltpu.VMEM((4, tiles, tok + qpart, lanes), bf16),
+            pltpu.VMEM((4, tiles, qpart, lanes), bf16),
+            pltpu.VMEM((4, tiles, qpart, lanes), bf16),
+            pltpu.VMEM((3, tok, width), bf16),
+            pltpu.VMEM((3, tok, width), bf16),
+            pltpu.VMEM((rows + 2, cols + 16, width), jnp.float32),
+            pltpu.VMEM((2, cols, width), bf16),
+            pltpu.VMEM((2, 16, width), bf16),
+            pltpu.VMEM((2, cols, width), bf16),
+            pltpu.VMEM((6, 16, width), bf16),
+            dma((3,)),
+            dma((3,)),
+            dma((3,)),
+            dma((4,)),
+            dma((4,)),
+            dma((4,)),
+            dma((4,)),
+            dma((3,)),
+            dma((3,)),
+            dma((8,)),
+            dma((8,)),
+        ],
+        compiler_params=pltpu.CompilerParams(
+            collective_id=0, has_side_effects=True, vmem_limit_bytes=48 * 2**20
+        ),
+        cost_estimate=pl.CostEstimate(
+            flops=2 * 10**9, bytes_accessed=5 * 10**6, transcendentals=2 * 10**6
+        ),
+    )(
+        bott,
+        norm_gain.reshape(1, width),
+        w_qkv,
+        w_out,
+        dw_weight,
+        join_bias.reshape(1, width),
+        w_join,
+    )
+
+
+def per_device_any(*args):
+    bott, w_qkv = args[0], args[2]
+    rows, cols, width = bott.shape
+    tiles = lax.axis_size("tile")
+    heads = w_qkv.shape[2] // (width // HEADS)
+    parts = tiles // heads
+    fits = (
+        lax.axis_size("head") == 4
+        and parts * heads == tiles
+        and heads % 2 == 0
+        and width == HEADS * 64
+        and rows == 2
+        and cols % 16 == 0
+        and (rows * cols) % (16 * parts) == 0
+    )
+    return fused(tiles, parts, *args) if fits else per_device(*args)
+
+
 def solution(mesh):
     placed = (P("tile", "head", None), P(), P(None, None, "head"), P("head", None), P(), P(), P())
     return jax.shard_map(
-        per_device, mesh=mesh, in_specs=placed, out_specs=P("tile", "head", None), check_vma=False
+        per_device_any, mesh=mesh, in_specs=placed, out_specs=P("tile", "head", None), check_vma=False
     )

time: 133 us -> 56.3 us (0.42)
  waiting for transfers between devices: 71.7 us -> 0 us
  Pallas kernels: 0 us -> 48.1 us
  blocking collectives: 15.3 us -> 0 us
  between operations: 13.3 us -> 0.02 us
  matrix products: 12.5 us -> 0 us
  starting transfers between devices: 9.97 us -> 0 us
  other arithmetic: 4.91 us -> 0 us
  local copies, waits for them, and re-layouts: 5.13 us -> 7.77 us
    pallas_call x0 -> x1, Pallas kernels: none -> 48.1 us  [fused(): pl.pallas_call(functools.partial(fused_kernel, tiles, parts), out_shape=j...]
    all_gather x2 -> x0, waiting for transfers between devices: 44.5 us -> none  [the longest x1 26.6 us: per_device(): key_piece = lax.all_gather(keys, 'tile', axis=0, tiled=True)]
    reduce_scatter x1 -> x0, waiting for transfers between devices: 19.6 us -> none  [per_device(): lax.psum_scatter(jnp.einsum('crh,hd->crd', attended, w_out, preferred_ele...]
    all_gather x1 -> x0, blocking collectives: 15.3 us -> none  [per_device(): gathered = lax.all_gather(normed, 'head', axis=1, tiled=True)]
    dot_general x5 -> x0, matrix products: 12.5 us -> none  [the longest x1 5.24 us: one_block(): jnp.einsum('hqk,khe->hqe', weights.astype(jnp.bfloat16), value_block, pre...]
    ppermute x4 -> x0, starting transfers between devices: 9.89 us -> none  [the longest x2 6.68 us: with_halo(): before = lax.ppermute(last, axis, up)]
    ppermute x4 -> x0, waiting for transfers between devices: 6.78 us -> none  [the longest x2 6.77 us: with_halo(): after = lax.ppermute(leading, axis, down)]
    unnamed x12 -> x15, local copies, waits for them, and re-layouts: 3.24 us -> 7.77 us
  transfers between devices with their start and end apart: 7 -> 0, of which waited for: 5 -> 0; matrix products, arithmetic and copies ran while one was open for 3% -> 0% of each run, Pallas kernels for 0% -> 0%
where the time goes in v2:
time: 56.3 us; the launch traced here: 55.9 us
  Pallas kernels  48.1 us (85%)
  local copies, waits for them, and re-layouts  7.77 us (14%)
    pallas_call x1, Pallas kernels, fused(): pl.pallas_call(functools.partial(fused_kernel, tiles, parts), out_shape=j...  48.1 us
    unnamed x15, local copies, waits for them, and re-layouts  7.77 us

profile of v2, /device:TPU:1, one launch (start us, length us, event | category | flops | bytes accessed | tf_op | source)
XLA Modules:
  0.0 55.9 jit_solution(14488569557028208698)
XLA Ops:
  0.0 0.0 copy-start
  0.0 1.6 %copy-done = bf16[1024,1024]{1,0:T(8,128)(2,1)S(1)} copy-done((bf16[1024,1024]{1,0:T(8,128)(2,1)S(1)}, bf16[1024,1024]{1,0:T(8,128)(2,1)}, u32[]{:S(2)}) %copy-start) | copy-done | bytes 2097176
  1.6 0.0 copy-start.1
  1.6 1.4 %copy-done.1 = bf16[3,1024,256]{2,1,0:T(8,128)(2,1)S(1)} copy-done((bf16[3,1024,256]{2,1,0:T(8,128)(2,1)S(1)}, bf16[3,1024,256]{2,1,0:T(8,128)(2,1)}, u32[]{:S(2)}) %copy-start.1) | copy-done | bytes 1572888
  3.0 0.0 copy-start.2
  3.0 1.0 %copy-done.2 = bf16[256,1024]{1,0:T(8,128)(2,1)S(1)} copy-done((bf16[256,1024]{1,0:T(8,128)(2,1)S(1)}, bf16[256,1024]{1,0:T(8,128)(2,1)}, u32[]{:S(2)}) %copy-start.2) | copy-done | bytes 524312
  4.0 0.0 copy-start.3
  4.0 0.9 %copy-done.3 = bf16[2,32,1024]{2,1,0:T(8,128)(2,1)S(1)} copy-done((bf16[2,32,1024]{2,1,0:T(8,128)(2,1)S(1)}, bf16[2,32,1024]{2,1,0:T(8,128)(2,1)}, u32[]{:S(2)}) %copy-start.3) | copy-done | bytes 131096
  4.9 0.0 copy-start.4
  4.9 0.8 %copy-done.4 = f32[3,3,1024]{2,1,0:T(4,128)S(1)} copy-done((f32[3,3,1024]{2,1,0:T(4,128)S(1)}, f32[3,3,1024]{2,1,0:T(4,128)}, u32[]{:S(2)}) %copy-start.4) | copy-done | bytes 36888
  5.7 0.0 copy-start.5
  5.7 0.7 %copy-done.5 = f32[1024]{0:T(1024)S(1)} copy-done((f32[1024]{0:T(1024)S(1)}, f32[1024]{0:T(1024)}, u32[]{:S(2)}) %copy-start.5) | copy-done | bytes 4120
  6.4 0.0 copy-start.6
  6.4 0.7 %copy-done.6 = f32[1024]{0:T(1024)S(1)} copy-done((f32[1024]{0:T(1024)S(1)}, f32[1024]{0:T(1024)}, u32[]{:S(2)}) %copy-start.6) | copy-done | bytes 4120
  7.1 48.1 %shard_map.73 = bf16[2,32,1024]{2,1,0:T(8,128)(2,1)S(1)} custom-call(bf16[2,32,1024]{2,1,0:T(8,128)(2,1)S(1)} %copy-done.3, f32[1,1024]{1,0:T(1,128)S(1)} %bitcast.2, bf16[3,1024,256]{2,1,0:T(8,128)(2,1)S(1)} %copy-done.1, bf16[256,1024]{1,0:T(8,128)(2,1)S(1)} %copy-done.2, f32[3,3,1024]{2,1,0:T(4,128)S(1)} %copy-done.4, f32[1,1024]{1,0:T(1,128)S(1)} %bitcast.3, ...), custom_call_target="tpu_custom_call" | custom-call | flops 2000000000 | bytes 5000000 | tf_op jit(solution)/shard_map/pallas_call | solution.py:416
  55.3 0.7 %copy.9 = bf16[2,32,1024]{2,1,0:T(8,128)(2,1)} copy(bf16[2,32,1024]{2,1,0:T(8,128)(2,1)S(1)} %shard_map.73) | data formatting | bytes 262144
Async XLA Ops:
  0.0 1.6 %copy-start = (bf16[1024,1024]{1,0:T(8,128)(2,1)S(1)}, bf16[1024,1024]{1,0:T(8,128)(2,1)}, u32[]{:S(2)}) copy-start(bf16[1024,1024]{1,0:T(8,128)(2,1)} %wjoin_hbm.1) | copy-start | bytes 6291460
  1.6 1.4 %copy-start.1 = (bf16[3,1024,256]{2,1,0:T(8,128)(2,1)S(1)}, bf16[3,1024,256]{2,1,0:T(8,128)(2,1)}, u32[]{:S(2)}) copy-start(bf16[3,1024,256]{2,1,0:T(8,128)(2,1)} %wqkv_hbm.1) | copy-start | bytes 4718596
  3.0 1.0 %copy-start.2 = (bf16[256,1024]{1,0:T(8,128)(2,1)S(1)}, bf16[256,1024]{1,0:T(8,128)(2,1)}, u32[]{:S(2)}) copy-start(bf16[256,1024]{1,0:T(8,128)(2,1)} %wout_hbm.1) | copy-start | bytes 1572868
  4.0 0.9 %copy-start.3 = (bf16[2,32,1024]{2,1,0:T(8,128)(2,1)S(1)}, bf16[2,32,1024]{2,1,0:T(8,128)(2,1)}, u32[]{:S(2)}) copy-start(bf16[2,32,1024]{2,1,0:T(8,128)(2,1)} %bott_ref.1) | copy-start | bytes 393220
  4.9 0.8 %copy-start.4 = (f32[3,3,1024]{2,1,0:T(4,128)S(1)}, f32[3,3,1024]{2,1,0:T(4,128)}, u32[]{:S(2)}) copy-start(f32[3,3,1024]{2,1,0:T(4,128)} %dw_ref.1) | copy-start | bytes 110596
  5.7 0.7 %copy-start.5 = (f32[1024]{0:T(1024)S(1)}, f32[1024]{0:T(1024)}, u32[]{:S(2)}) copy-start(f32[1024]{0:T(1024)} %param.8) | copy-start | bytes 12292
  6.4 0.7 %copy-start.6 = (f32[1024]{0:T(1024)S(1)}, f32[1024]{0:T(1024)}, u32[]{:S(2)}) copy-start(f32[1024]{0:T(1024)} %param.12) | copy-start | bytes 12292

commit v3 on v2

--- a/solution.py
+++ b/solution.py
@@ -118,14 +118,18 @@
 def fused_kernel(
     tiles,
     parts,
+    bott_hbm,
+    gain_hbm,
+    wqkv_hbm,
+    wout_hbm,
+    dw_hbm,
+    bias_hbm,
+    wjoin_hbm,
+    out_ref,
     bott_ref,
     gain_ref,
-    wqkv_hbm,
-    wout_hbm,
     dw_ref,
     bias_ref,
-    wjoin_hbm,
-    out_ref,
     wqkv,
     wout,
     wjoin,
@@ -139,6 +143,7 @@
     pad,
     hrow_s,
     hcol_s,
+    hcol_f,
     hrow,
     hcol,
     wsem,
@@ -175,7 +180,13 @@
         pltpu.make_async_copy(wout_hbm, wout, wsem.at[1]),
         pltpu.make_async_copy(wjoin_hbm, wjoin, wsem.at[2]),
     ]
-    for load in loads:
+    small = [
+        pltpu.make_async_copy(bott_hbm, bott_ref, wsem.at[3]),
+        pltpu.make_async_copy(gain_hbm, gain_ref, wsem.at[4]),
+        pltpu.make_async_copy(dw_hbm, dw_ref, wsem.at[5]),
+        pltpu.make_async_copy(bias_hbm, bias_ref, wsem.at[6]),
+    ]
+    for load in small[:2]:
         load.start()
 
     barrier = pltpu.get_barrier_semaphore()
@@ -192,6 +203,10 @@
         for dz in (zleft, zright):
             pl.semaphore_signal(barrier, inc=1, device_id=(dt, dz), device_id_type=MESH)
 
+    for load in loads + small[2:]:
+        load.start()
+    for load in small[:2]:
+        load.wait()
     values = bott_ref[...].reshape(tok, width).astype(f32)
     mean = jnp.mean(values * values, axis=-1, keepdims=True)
     nrm[0] = (values * lax.rsqrt(mean + 1e-06) * gain_ref[...]).astype(bf16)
@@ -199,18 +214,25 @@
 
     pl.semaphore_wait(barrier, 3 + (tiles - 1) + 4)
 
-    ncopies = []
-    for k in (1, 2, 3):
+    half = tok // 2
+    ncopies = {}
+
+    def pass_block(src, dst, k, n, part):
         copy = pltpu.make_async_remote_copy(
-            src_ref=nrm.at[0],
-            dst_ref=nrm.at[k],
-            send_sem=nsend.at[k - 1],
-            recv_sem=nrecv.at[k - 1],
+            src_ref=nrm.at[src, part],
+            dst_ref=nrm.at[dst, part],
+            send_sem=nsend.at[n],
+            recv_sem=nrecv.at[n],
             device_id=(t, zpeer(k)),
             device_id_type=MESH,
         )
         copy.start()
-        ncopies.append(copy)
+        ncopies[n] = copy
+
+    halves = (pl.ds(0, half), pl.ds(half, half))
+    for n in (0, 1):
+        pass_block(0, 2, 2, n, halves[n])
+    pass_block(0, 1, 1, 4, pl.ds(0, tok))
     loads[0].wait()
 
     low = lax.broadcasted_iota(jnp.int32, (tok, 2 * head_dim), 1) < head_dim
@@ -221,9 +243,16 @@
     def all_of(ref, sem):
         pltpu.make_async_copy(ref, ref, sem).wait()
 
-    for k in range(4):
-        if k > 0:
-            ncopies[k - 1].wait_recv()
+    for k in (0, 2, 1, 3):
+        if k == 2:
+            for n in (0, 1):
+                ncopies[n].wait_recv()
+                pass_block(2, 3, 1, 2 + n, halves[n])
+        elif k == 1:
+            ncopies[4].wait_recv()
+        elif k == 3:
+            for n in (2, 3):
+                ncopies[n].wait_recv()
         x = nrm[k]
         q = jnp.dot(x, wqkv[0], preferred_element_type=f32) * scale
         key = jnp.dot(x, wqkv[1], preferred_element_type=f32)
@@ -332,11 +361,14 @@
     pad[1 : rows + 1, 8 : 8 + cols] = wide
     hrow_s[0] = narrow[0]
     hrow_s[1] = narrow[rows - 1]
-    first_row = lax.broadcasted_iota(jnp.int32, (16, width), 0) == 0
+    strips = width // 128
     for side, c in ((0, 0), (1, cols - 1)):
-        hcol_s[side] = jnp.where(
-            first_row, wide[0, c : c + 1], wide[rows - 1, c : c + 1]
-        ).astype(bf16)
+        for r in range(rows):
+            for n in range(strips):
+                hcol_f[side, r * strips + n : r * strips + n + 1] = wide[
+                    r, c : c + 1, n * 128 : (n + 1) * 128
+                ]
+        hcol_s[side] = hcol_f[side].astype(bf16)
 
     hcopies = []
     plan = [
@@ -360,9 +392,10 @@
         )
         copy.start()
         hcopies.append(copy)
-    loads[2].wait()
-
-    for copy in ncopies:
+    for load in [loads[2]] + small[2:]:
+        load.wait()
+
+    for copy in ncopies.values():
         copy.wait_send()
     for k in range(4):
         all_of(snd.at[k, pl.ds(0, tiles - 1)], qsend.at[k])
@@ -381,12 +414,13 @@
     pad[rows + 1, 8:end] = hrow[1].astype(f32) * down_ok
     for n, ok, at in ((0, left_ok, 7), (1, right_ok, end)):
         column = hcol[n].astype(f32) * ok
-        pad[1, at : at + 1] = column[0:1]
-        pad[2, at : at + 1] = column[1:2]
         above = hcol[2 + n].astype(f32) * (ok * up_ok)
-        pad[0, at : at + 1] = above[1:2]
         below = hcol[4 + n].astype(f32) * (ok * down_ok)
-        pad[rows + 1, at : at + 1] = below[0:1]
+        for row, cells, r in ((1, column, 0), (2, column, 1), (0, above, 1), (3, below, 0)):
+            for m in range(strips):
+                pad[row, at : at + 1, m * 128 : (m + 1) * 128] = cells[
+                    r * strips + m : r * strips + m + 1
+                ]
 
     total = context.astype(f32)
     step = 256
@@ -411,14 +445,18 @@
     qpart = tok // parts
     bf16 = jnp.bfloat16
     vmem = pl.BlockSpec(memory_space=pltpu.VMEM)
-    hbm = pl.BlockSpec(memory_space=pl.ANY)
+    hbm = pl.BlockSpec(memory_space=pltpu.HBM)
     dma = pltpu.SemaphoreType.DMA
     return pl.pallas_call(
         functools.partial(fused_kernel, tiles, parts),
         out_shape=jax.ShapeDtypeStruct(bott.shape, bf16),
-        in_specs=[vmem, vmem, hbm, hbm, vmem, vmem, hbm],
+        in_specs=[hbm] * 7,
         out_specs=vmem,
         scratch_shapes=[
+            pltpu.VMEM(bott.shape, bf16),
+            pltpu.VMEM((1, width), jnp.float32),
+            pltpu.VMEM(dw_weight.shape, jnp.float32),
+            pltpu.VMEM((1, width), jnp.float32),
             pltpu.VMEM(w_qkv.shape, bf16),
             pltpu.VMEM(w_out.shape, bf16),
             pltpu.VMEM(w_join.shape, bf16),
@@ -431,12 +469,13 @@
             pltpu.VMEM((3, tok, width), bf16),
             pltpu.VMEM((rows + 2, cols + 16, width), jnp.float32),
             pltpu.VMEM((2, cols, width), bf16),
-            pltpu.VMEM((2, 16, width), bf16),
+            pltpu.VMEM((2, rows * width // 128, 128), bf16),
+            pltpu.VMEM((2, rows * width // 128, 128), jnp.float32),
             pltpu.VMEM((2, cols, width), bf16),
-            pltpu.VMEM((6, 16, width), bf16),
-            dma((3,)),
-            dma((3,)),
-            dma((3,)),
+            pltpu.VMEM((6, rows * width // 128, 128), bf16),
+            dma((7,)),
+            dma((5,)),
+            dma((5,)),
             dma((4,)),
             dma((4,)),
             dma((4,)),
@@ -447,7 +486,7 @@
             dma((8,)),
         ],
         compiler_params=pltpu.CompilerParams(
-            collective_id=0, has_side_effects=True, vmem_limit_bytes=48 * 2**20
+            collective_id=0, has_side_effects=True, vmem_limit_bytes=56 * 2**20
         ),
         cost_estimate=pl.CostEstimate(
             flops=2 * 10**9, bytes_accessed=5 * 10**6, transcendentals=2 * 10**6

time: 56.3 us -> 46.5 us (0.83)
  local copies, waits for them, and re-layouts: 7.77 us -> 1.57 us
  Pallas kernels: 48.1 us -> 44.7 us
    unnamed x15 -> x1, local copies, waits for them, and re-layouts: 7.77 us -> 1.57 us
    pallas_call x1, Pallas kernels: 48.1 us -> 44.7 us  [fused(): pl.pallas_call(functools.partial(fused_kernel, tiles, parts), out_shape=j...]
where the time goes in v3:
time: 46.5 us; the launch traced here: 46.3 us
  Pallas kernels  44.7 us (96%)
  local copies, waits for them, and re-layouts  1.57 us (3%)
    pallas_call x1, Pallas kernels, fused(): pl.pallas_call(functools.partial(fused_kernel, tiles, parts), out_shape=j...  44.7 us
    unnamed x1, local copies, waits for them, and re-layouts  1.57 us

profile of v3, /device:TPU:1, one launch (start us, length us, event | category | flops | bytes accessed | tf_op | source)
XLA Modules:
  0.0 46.3 jit_solution(2315295193284421483)
XLA Ops:
  0.0 44.7 %shard_map.73 = bf16[2,32,1024]{2,1,0:T(8,128)(2,1)} custom-call(bf16[2,32,1024]{2,1,0:T(8,128)(2,1)} %bott_hbm.1, f32[1,1024]{1,0:T(1,128)} %bitcast.2, bf16[3,1024,256]{2,1,0:T(8,128)(2,1)} %wqkv_hbm.1, bf16[256,1024]{1,0:T(8,128)(2,1)} %wout_hbm.1, f32[3,3,1024]{2,1,0:T(4,128)} %dw_hbm.1, f32[1,1024]{1,0:T(1,128)} %bitcast.3, bf16[1024,1024]{1,0:T(8,128)(2,1)} %wjoin_hbm.1), custom_call_target="tpu_custom_call" | custom-call | flops 2000000000 | bytes 5000000 | tf_op jit(solution)/shard_map/pallas_call | solution.py:450
  44.7 1.6 %copy.9 = bf16[2,32,1024]{2,1,0:T(8,128)(2,1)} copy(bf16[2,32,1024]{2,1,0:T(8,128)(2,1)} %shard_map.73) | data formatting | bytes 262144

commit v4 on v3

--- a/solution.py
+++ b/solution.py
@@ -286,12 +286,9 @@
 
         rcv[k, t] = snd[k, t]
 
-    for k in range(4):
-        all_of(rcv.at[k, pl.ds(0, tiles - 1)], qrecv.at[k])
-
     loads[1].wait()
-    order = (3, 2, 1, 0)
-    kvs = [rcv[k, :, :tok].reshape(tiles * tok, lanes) for k in range(4)]
+    order = (2, 3, 1, 0)
+    kvs = []
     own = [None]
 
     def project(k):
@@ -320,11 +317,21 @@
 
     pcopies = []
     for step, k in enumerate(order):
+        if step == 0:
+            for n in (0, 2):
+                all_of(rcv.at[n, pl.ds(0, tiles - 1)], qrecv.at[n])
         qs = rcv[k, :, tok:].reshape(tiles * qpart, lanes)
-        scores = [
-            lax.dot_general(qs, kv, (((1,), (1,)), ((), ())), preferred_element_type=f32)
-            for kv in kvs
-        ]
+        scores = []
+        for i, n in enumerate((0, 2, 1, 3)):
+            if step == 0:
+                if i > 1:
+                    all_of(rcv.at[n, pl.ds(0, tiles - 1)], qrecv.at[n])
+                kvs.append(rcv[n, :, :tok].reshape(tiles * tok, lanes))
+            scores.append(
+                lax.dot_general(
+                    qs, kvs[i], (((1,), (1,)), ((), ())), preferred_element_type=f32
+                )
+            )
         top = functools.reduce(jnp.maximum, [jnp.max(s, axis=-1, keepdims=True) for s in scores])
         total, summed = 0.0, 0.0
         for s, kv in zip(scores, kvs):

time: 46.5 us -> 45.7 us (0.983)
  Pallas kernels: 44.7 us -> 44 us
    pallas_call x1, Pallas kernels: 44.7 us -> 44 us  [fused(): pl.pallas_call(functools.partial(fused_kernel, tiles, parts), out_shape=j...]
where the time goes in v4:
time: 45.7 us; the launch traced here: 45.6 us
  Pallas kernels  44 us (96%)
  local copies, waits for them, and re-layouts  1.57 us (3%)
    pallas_call x1, Pallas kernels, fused(): pl.pallas_call(functools.partial(fused_kernel, tiles, parts), out_shape=j...  44 us
    unnamed x1, local copies, waits for them, and re-layouts  1.57 us

profile of v4, /device:TPU:1, one launch (start us, length us, event | category | flops | bytes accessed | tf_op | source)
XLA Modules:
  0.0 45.6 jit_solution(16989004969967440474)
XLA Ops:
  0.0 44.0 %shard_map.73 = bf16[2,32,1024]{2,1,0:T(8,128)(2,1)} custom-call(bf16[2,32,1024]{2,1,0:T(8,128)(2,1)} %bott_hbm.1, f32[1,1024]{1,0:T(1,128)} %bitcast.2, bf16[3,1024,256]{2,1,0:T(8,128)(2,1)} %wqkv_hbm.1, bf16[256,1024]{1,0:T(8,128)(2,1)} %wout_hbm.1, f32[3,3,1024]{2,1,0:T(4,128)} %dw_hbm.1, f32[1,1024]{1,0:T(1,128)} %bitcast.3, bf16[1024,1024]{1,0:T(8,128)(2,1)} %wjoin_hbm.1), custom_call_target="tpu_custom_call" | custom-call | flops 2000000000 | bytes 5000000 | tf_op jit(solution)/shard_map/pallas_call | solution.py:457
  44.0 1.6 %copy.9 = bf16[2,32,1024]{2,1,0:T(8,128)(2,1)} copy(bf16[2,32,1024]{2,1,0:T(8,128)(2,1)} %shard_map.73) | data formatting | bytes 262144
